TPU v7x, 512 devices: a whole 4x4x16 slice. The times are simulated.
512 devices in a mesh: row: 32 (over x_hi, z), col: 16 (over y, x_lo, core).
Axes of the slice: x: 4 (x_hi: 2, x_lo: 2; x = x_hi * 2 + x_lo), y: 4, z: 16, core: 2. Of those that a mesh axis runs over, the one named last changes fastest.
Arguments:
- pair_elements: bfloat16 [1024, 61440], P(('row', 'col')), may hold values from -6 to 6
- energy_gaps: float32 [1024], replicated, may hold values from 0.5 to 3
- frequencies: float32 [3], replicated, may hold values from 0.3 to 3
Outputs:
- polarizability: bfloat16 [3, 4096, 61440], P(None, 'row', 'col')
All inputs are finite; a program needn't handle non-finite values.
Results may differ from a plain program's by a relative error of at most 0.0048.
Values may be sent and summed in bfloat16 or wider, within the bound.
A program may use at most 64 MiB of HBM per device.

v0:
```python
import functools
import math

import jax
import jax.numpy as jnp
from jax import lax
from jax.experimental import pallas as pl
from jax.experimental.pallas import tpu as pltpu
from jax.sharding import PartitionSpec as P

NW = 3
GSR = 128
OWN = (640, 896)
LENT = (640, 512)
MESH = pl.DeviceIdType.MESH


def kernel(nz, ny, pairs, elements, gaps_in, freqs_in, out, gaps, turned_gaps, weights, freqs,
           packed_a, packed_b, parts_a, parts_b, own_a, own_b, lent_a, lent_b, got_a, got_b, wbuf, lhs,
           out_own_a, out_own_b, out_a, out_b, in_sem, pack_sem, part_recv, part_send,
           zrecv, zsend, xrecv, xsend, wrecv, wsend, osem):
    row, col = lax.axis_index("row"), lax.axis_index("col")
    hi, z = row // nz, lax.rem(row, nz)
    ncol = ny * 4
    plane = 2 * ncol
    seat = hi * ncol + col
    y = col // 4
    in_y = lax.rem(col, 4)
    lo, core = in_y // 2, lax.rem(in_y, 2)
    up = (hi * nz + lax.rem(z + 1, nz), col)
    down = (hi * nz + lax.rem(z + nz - 1, nz), col)
    other_lo = y * 4 + (1 - lo) * 2 + core
    side = [(z, other_lo), (nz + z, other_lo)]
    in_column = [(row, lax.rem(y + k, ny) * 4 + in_y) for k in (1, 3, 2)]
    twin_lo = (row, other_lo)
    twin_core = (row, y * 4 + lo * 2 + (1 - core))
    half = nz // 2

    def seated(k):
        to = lax.rem(seat + k, plane)
        return to // ncol, lax.rem(to, ncol) // 4, lax.rem(to, 4) // 2, lax.rem(to, 2)

    def device_at(h, y, lo, core):
        return h * nz + z, y * 4 + lo * 2 + core

    barrier = pltpu.get_barrier_semaphore()
    for device in (up, down):
        pl.semaphore_signal(barrier, inc=1, device_id=device, device_id_type=MESH)

    @pl.loop(1, plane)
    def _(k):
        pl.semaphore_signal(barrier, inc=1, device_id=device_at(*seated(k)), device_id_type=MESH)

    packing = []
    for n, packed in enumerate((packed_a, packed_b)):
        lent_at, own_at = sum(LENT[:n]), sum(OWN[:n])
        for h in range(2):
            for to in range(2):
                packing.append(pltpu.make_async_copy(
                    elements.at[:, 1 - to, :, :, pl.ds(sum(OWN) + h * sum(LENT) + lent_at, LENT[n])],
                    packed.at[h, :, to, :, :, pl.ds(0, LENT[n])], pack_sem.at[n, 2 * h + to],
                ))
            packing.append(pltpu.make_async_copy(
                elements.at[:, :, :, :, pl.ds(own_at, OWN[n])],
                packed.at[h, :, :, :, :, pl.ds(LENT[n], OWN[n])], pack_sem.at[n, 4 + h],
            ))
    for copy in packing:
        copy.start()
    loads = [
        pltpu.make_async_copy(gaps_in, gaps, in_sem.at[0]),
        pltpu.make_async_copy(freqs_in, freqs, in_sem.at[1]),
    ]
    for load in loads:
        load.start()

    for copy in packing[:6]:
        copy.wait()
    pl.semaphore_wait(barrier, plane + 1)

    def remote(src, dst, send, recv, device):
        return pltpu.make_async_remote_copy(
            src_ref=src, dst_ref=dst, send_sem=send, recv_sem=recv, device_id=device, device_id_type=MESH
        )

    def wait(ref, sem):
        pltpu.make_async_copy(ref, ref, sem).wait()

    def exchange(n):
        packed, parts = ((packed_a, parts_a), (packed_b, parts_b))[n]

        @pl.loop(1, plane)
        def _(k):
            to = seated(k)
            remote(packed.at[to], parts.at[seat], part_send.at[n], part_recv.at[n], device_at(*to)).start()

        parts[seat] = packed[hi, y, lo, core]

    exchange(0)

    for load in loads:
        load.wait()
    for k in range(4):
        turned_gaps[k] = pltpu.roll(gaps[...], k * 32, 1)
    quarter = lax.broadcasted_iota(jnp.int32, (1, GSR), 1) // 32

    @pl.loop(0, pairs // GSR)
    def _(b):
        line = jnp.zeros((1, GSR), jnp.float32)
        for q in range(4):
            at = lax.rem(b, 4) * 4 + q
            away = (at + 1) // 2 if q % 2 == 0 else nz - (at + 1) // 2
            if q % 2 == 1:
                away = lax.rem(away, nz)
            plane_at = lax.rem(z + away, nz)
            shift = lax.rem(q + 4 - lax.rem(plane_at, 4), 4)
            piece = turned_gaps[shift, pl.ds(b // 4 * 4 + plane_at // 4, 1), :]
            line = jnp.where(quarter == q, piece, line)
        for w in range(NW):
            weights[w, pl.ds(b, 1), :] = (
                -4.0 * line / ((line * line + freqs[w] * freqs[w]) * math.sqrt(pairs))
            )

    bufs = (own_a, own_b, lent_a, lent_b)
    got = (got_a, got_b)
    rounds = ((2, 0), (3, 1))

    def begin(chunk):
        n, parts = chunk % 2, (parts_a, parts_b)[chunk % 2]
        start, width = (0, LENT[n]) if chunk >= 2 else (LENT[n], OWN[n])
        for h in range(2):
            part = parts[h * ncol:(h + 1) * ncol, :, start:start + width]
            bufs[chunk][h, 0] = part.reshape(2 * ncol, width)

    def place(way, s):
        return 2 * s - 1 + way

    def push(chunk, first, count):
        j = chunk - 2
        for n in range(2):
            remote(
                bufs[chunk].at[:, pl.ds(first, count)], got[j].at[hi, :, pl.ds(first, count)],
                xsend.at[n, j], xrecv.at[hi, j], side[n],
            ).start()

    def arrived(chunk, h, way, s):
        at = place(way, s) if not isinstance(s, int) or s < half else nz - 1
        wait(bufs[chunk].at[h, at], zrecv.at[way, chunk, h, s - 1])

    def tick(chunk, h, s):
        first, final = isinstance(s, int) and s == 0, isinstance(s, int) and s == half - 1
        buf = bufs[chunk]
        for way, device in ((0, up), (1, down)):
            if not first:
                arrived(chunk, h, way, s)
            if final and way != h:
                continue
            src = 0 if first else place(way, s)
            dst = nz - 1 if final else place(way, s + 1)
            remote(
                buf.at[h, src], buf.at[h, dst],
                zsend.at[way, chunk, h], zrecv.at[way, chunk, h, s], device,
            ).start()

    def last(chunk):
        for h in range(2):
            arrived(chunk, h, h, half)
        if chunk >= 2:
            push(chunk, nz - 1, 1)

    def ticks(n, low, high):
        def one(s):
            for chunk in rounds[n]:
                for h in range(2):
                    tick(chunk, h, s)
            push(rounds[n][0], place(0, s), 2)

        if high - low == 1:
            one(low)
        else:
            pl.loop(low, high)(one)

    window_col = row // 2
    in_w = lax.rem(window_col, 4)
    same_core = core == lax.rem(in_w, 2)
    same_line = jnp.logical_and(same_core, lo == in_w // 2)
    is_source = jnp.logical_and(same_line, y == window_col // 4)

    def window_y():
        @pl.when(is_source)
        def _():
            for b in range(2):
                @pl.when(lax.rem(row, 2) == b)
                def _():
                    wbuf[...] = own_a[:, :, :, b * GSR:(b + 1) * GSR]
            for k, device in enumerate(in_column):
                remote(wbuf, wbuf, wsend.at[k], wrecv.at[0], device).start()

    def window_x():
        @pl.when(same_line)
        def _():
            @pl.when(jnp.logical_not(is_source))
            def _():
                wait(wbuf, wrecv.at[0])
            remote(wbuf, wbuf, wsend.at[ny - 1], wrecv.at[1], twin_lo).start()

    def window_core():
        @pl.when(same_core)
        def _():
            @pl.when(jnp.logical_not(same_line))
            def _():
                wait(wbuf, wrecv.at[1])
            remote(wbuf, wbuf, wsend.at[ny], wrecv.at[2], twin_core).start()

    def window_done():
        @pl.when(jnp.logical_not(same_core))
        def _():
            wait(wbuf, wrecv.at[2])

        @pl.loop(0, pairs // GSR)
        def _(b):
            at = pl.multiple_of(b * GSR, GSR)
            block = wbuf[b // 4, pl.ds(lax.rem(b, 4) * 4, 4)].reshape(GSR, GSR)
            turned = block.astype(jnp.float32).T
            for w in range(NW):
                lhs[w * GSR:(w + 1) * GSR, pl.ds(at, GSR)] = (
                    turned * weights[w, pl.ds(b, 1), :]
                ).astype(jnp.bfloat16)

    def multiply(buf, to, at, sem):
        width = buf.shape[-1]
        chi = jnp.dot(lhs[...], buf[...].reshape(pairs, width), preferred_element_type=jnp.float32)
        to[...] = chi.astype(jnp.bfloat16).reshape(NW, GSR, width)
        write(to, at, sem).start()

    def write(to, at, sem):
        return pltpu.make_async_copy(to, out.at[:, :, pl.ds(at, to.shape[-1])], osem.at[sem])

    def place_of(h, j):
        return pl.multiple_of(sum(OWN) + h * sum(LENT) + j * LENT[0], 128)

    for n, (lent, own) in enumerate(rounds):
        parts = (parts_a, parts_b)[n]
        wait(parts.at[pl.ds(0, plane - 1)], part_recv.at[n])
        for chunk in (lent, own):
            begin(chunk)
            for h in range(2):
                tick(chunk, h, 0)
            if chunk == lent:
                push(chunk, 0, 1)
        if n == 0:
            for copy in packing[6:]:
                copy.wait()
            exchange(1)
            ticks(0, 1, half - 1)
        else:
            for chunk in rounds[0]:
                last(chunk)
            window_y()
            ticks(1, 1, 4)
            window_x()
            ticks(1, 4, 6)
            window_core()
            ticks(1, 6, half - 1)
            window_done()
        ticks(n, half - 1, half)

    multiply(own_a, out_own_a, 0, 0)
    last(3)
    for j in range(2):
        if j == 1:
            last(1)
            multiply(own_b, out_own_b, OWN[0], 1)

        @pl.loop(0, 2)
        def _(h):
            wait(got[j].at[h], xrecv.at[h, j])
            multiply(got[j].at[h], (out_a, out_b)[j].at[h], place_of(h, j), 2 + 2 * j + h)

    for chunk in range(4):
        for way in range(2):
            for h in range(2):
                wait(bufs[chunk].at[h, pl.ds(0, half if way == h else half - 1)], zsend.at[way, chunk, h])
    for j in range(2):
        for n in range(2):
            wait(bufs[2 + j], xsend.at[n, j])
    for n, parts in enumerate((parts_a, parts_b)):
        wait(parts.at[pl.ds(0, plane - 1)], part_send.at[n])

    @pl.when(is_source)
    def _():
        for k in range(ny - 1):
            wait(wbuf, wsend.at[k])

    @pl.when(same_line)
    def _():
        wait(wbuf, wsend.at[ny - 1])

    @pl.when(same_core)
    def _():
        wait(wbuf, wsend.at[ny])

    write(out_own_a, 0, 0).wait()
    write(out_own_b, OWN[0], 1).wait()
    for j in range(2):
        for h in range(2):
            write((out_a, out_b)[j].at[h], place_of(h, j), 2 + 2 * j + h).wait()


def on_device(pair_elements, energy_gaps, frequencies):
    rows, cols = lax.axis_size("row"), lax.axis_size("col")
    local, full = pair_elements.shape
    pairs = local * rows * cols
    block = full // cols
    nz, ny = rows // 2, cols // 4
    depth = local * cols
    plane = 2 * cols
    dma = pltpu.SemaphoreType.DMA

    def panels(*shape):
        return pltpu.VMEM(shape[:-1] + (2, nz, depth) + shape[-1:], jnp.bfloat16)

    def results(*shape):
        return pltpu.VMEM(shape[:-1] + (NW, GSR) + shape[-1:], jnp.bfloat16)

    operands = [
        pltpu.with_memory_space_constraint(operand, pltpu.HBM)
        for operand in (
            pair_elements.reshape(local, ny, 2, 2, block).transpose(1, 2, 3, 0, 4),
            energy_gaps.reshape(pairs // GSR, GSR),
            frequencies,
        )
    ]
    return pl.pallas_call(
        functools.partial(kernel, nz, ny, pairs),
        out_shape=jax.ShapeDtypeStruct((NW, GSR, block), jnp.bfloat16),
        in_specs=[pl.BlockSpec(memory_space=pl.ANY)] * 3,
        out_specs=pl.BlockSpec(memory_space=pl.ANY),
        scratch_shapes=[
            pltpu.VMEM((pairs // GSR, GSR), jnp.float32),
            pltpu.VMEM((4, pairs // GSR, GSR), jnp.float32),
            pltpu.VMEM((NW, pairs // GSR, GSR), jnp.float32),
            pltpu.SMEM((NW,), jnp.float32),
            pltpu.VMEM((2, ny, 2, 2, local, LENT[0] + OWN[0]), jnp.bfloat16),
            pltpu.VMEM((2, ny, 2, 2, local, LENT[1] + OWN[1]), jnp.bfloat16),
            pltpu.VMEM((plane, local, LENT[0] + OWN[0]), jnp.bfloat16),
            pltpu.VMEM((plane, local, LENT[1] + OWN[1]), jnp.bfloat16),
            panels(OWN[0]),
            panels(OWN[1]),
            panels(LENT[0]),
            panels(LENT[1]),
            panels(2, LENT[0]),
            panels(2, LENT[1]),
            pltpu.VMEM((2, nz, depth, GSR), jnp.bfloat16),
            pltpu.VMEM((NW * GSR, pairs), jnp.bfloat16),
            results(OWN[0]),
            results(OWN[1]),
            results(2, LENT[0]),
            results(2, LENT[1]),
            dma((2,)),
            dma((2, 6)),
            dma((2,)),
            dma((2,)),
            dma((2, 4, 2, nz // 2)),
            dma((2, 4, 2)),
            dma((2, 2)),
            dma((2, 2)),
            dma((3,)),
            dma((ny + 1,)),
            dma((6,)),
        ],
        compiler_params=pltpu.CompilerParams(
            collective_id=0, has_side_effects=True, vmem_limit_bytes=36 * 1024 * 1024
        ),
        cost_estimate=pl.CostEstimate(
            flops=2 * NW * GSR * pairs * block, bytes_accessed=2 * NW * GSR * block, transcendentals=0
        ),
    )(*operands)


def solution(mesh):
    in_specs = (P(("row", "col"), None), P(), P())
    out_specs = P(None, "row", "col")
    return jax.shard_map(
        on_device, mesh=mesh, in_specs=in_specs, out_specs=out_specs, check_vma=False
    )
```

profile of v0, /device:TPU:32, one launch (start us, length us, event | category | flops | bytes accessed | tf_op | source)
XLA Modules:
  0.0 86.2 jit_solution(12321606405795487203)
XLA Ops:
  0.0 84.6 %shard_map.37 = bf16[3,128,3840]{2,1,0:T(8,128)(2,1)S(1)} custom-call(bf16[4,2,2,2,3840]{4,3,2,1,0:T(2,128)(2,1)} %bitcast.4, f32[8,128]{1,0:T(8,128)} %bitcast.5, f32[3]{0:T(128)} %freqs_in.1), custom_call_target="tpu_custom_call" | custom-call | flops 3019898880 | bytes 2949120 | tf_op jit(solution)/shard_map/pallas_call | solution.py:333
  84.6 1.6 %copy.5 = bf16[3,128,3840]{2,1,0:T(8,128)(2,1)} copy(bf16[3,128,3840]{2,1,0:T(8,128)(2,1)S(1)} %shard_map.37) | data formatting | bytes 5898240
where the time goes:
time: 86.4 us; the launch traced here: 86.2 us
  Pallas kernels  84.6 us (98%)
  local copies, waits for them, and re-layouts  1.6 us (2%)
    pallas_call x1, Pallas kernels, on_device(): pl.pallas_call(functools.partial(kernel, nz, ny, pairs), out_shape=jax.Sh...  84.6 us

commit v1 on v0

v1 whole, which is shorter than its diff:
```python
import functools
import math

import jax
import jax.numpy as jnp
from jax import lax
from jax.experimental import pallas as pl
from jax.experimental.pallas import tpu as pltpu
from jax.sharding import PartitionSpec as P

NW = 3
GSR = 128
WINDOW = 256
OWN = 1280
LENT = 1152
EARLY = 12
MESH = pl.DeviceIdType.MESH


def kernel(nz, ny, pairs, elements, gaps_in, freqs_in, out, gaps, turned_gaps, weights, freqs,
           packed_a, packed_b, parts_a, parts_b, win, own, lent, got, wbuf, lhs,
           sum_own, sum_got, out_win, out_own, out_got, in_sem, pack_sem, part_recv, part_send,
           nrecv, nsend, zrecv, zsend, xrecv, xsend, wrecv, wsend, osem):
    row, col = lax.axis_index("row"), lax.axis_index("col")
    hi, z = row // nz, lax.rem(row, nz)
    ncol = ny * 4
    plane = 2 * ncol
    seat = hi * ncol + col
    y = col // 4
    in_y = lax.rem(col, 4)
    lo, core = in_y // 2, lax.rem(in_y, 2)
    up = (hi * nz + lax.rem(z + 1, nz), col)
    down = (hi * nz + lax.rem(z + nz - 1, nz), col)
    other_lo = y * 4 + (1 - lo) * 2 + core
    side = [(z, other_lo), (nz + z, other_lo)]
    in_column = [(row, lax.rem(y + k, ny) * 4 + in_y) for k in (1, 3, 2)]
    twin_lo = (row, other_lo)
    twin_core = (row, y * 4 + lo * 2 + (1 - core))
    half = nz // 2

    def seated(k):
        to = lax.rem(seat + k, plane)
        return to // ncol, lax.rem(to, ncol) // 4, lax.rem(to, 4) // 2, lax.rem(to, 2)

    def device_at(h, y, lo, core):
        return h * nz + z, y * 4 + lo * 2 + core

    barrier = pltpu.get_barrier_semaphore()
    for device in (up, down):
        pl.semaphore_signal(barrier, inc=1, device_id=device, device_id_type=MESH)

    @pl.loop(1, plane)
    def _(k):
        pl.semaphore_signal(barrier, inc=1, device_id=device_at(*seated(k)), device_id_type=MESH)

    packing = []
    for h in range(2):
        for to in range(2):
            packing.append(pltpu.make_async_copy(
                elements.at[:, 1 - to, :, :, pl.ds(WINDOW + OWN + h * LENT, LENT)],
                packed_a.at[h, :, to, :, :, pl.ds(WINDOW, LENT)], pack_sem.at[2 * h + to],
            ))
        packing.append(pltpu.make_async_copy(
            elements.at[:, :, :, :, pl.ds(0, WINDOW)],
            packed_a.at[h, :, :, :, :, pl.ds(0, WINDOW)], pack_sem.at[4 + h],
        ))
    for h in range(2):
        packing.append(pltpu.make_async_copy(
            elements.at[:, :, :, :, pl.ds(WINDOW, OWN)], packed_b.at[h], pack_sem.at[6 + h],
        ))
    for copy in packing:
        copy.start()
    loads = [
        pltpu.make_async_copy(gaps_in, gaps, in_sem.at[0]),
        pltpu.make_async_copy(freqs_in, freqs, in_sem.at[1]),
    ]
    for load in loads:
        load.start()

    for copy in packing[:6]:
        copy.wait()
    pl.semaphore_wait(barrier, plane + 1)

    def remote(src, dst, send, recv, device):
        return pltpu.make_async_remote_copy(
            src_ref=src, dst_ref=dst, send_sem=send, recv_sem=recv, device_id=device, device_id_type=MESH
        )

    def wait(ref, sem):
        pltpu.make_async_copy(ref, ref, sem).wait()

    def exchange(n):
        packed, parts = ((packed_a, parts_a), (packed_b, parts_b))[n]

        @pl.loop(1, plane)
        def _(k):
            to = seated(k)
            remote(packed.at[to], parts.at[seat], part_send.at[n], part_recv.at[n], device_at(*to)).start()

        parts[seat] = packed[hi, y, lo, core]

    exchange(0)

    for load in loads:
        load.wait()
    for k in range(4):
        turned_gaps[k] = pltpu.roll(gaps[...], k * 32, 1)
    quarter = lax.broadcasted_iota(jnp.int32, (1, GSR), 1) // 32

    @pl.loop(0, pairs // GSR)
    def _(b):
        line = jnp.zeros((1, GSR), jnp.float32)
        for q in range(4):
            plane_at = lax.rem(z + (b if q < 2 else nz - 1 - b), nz)
            shift = lax.rem(q + 4 - lax.rem(plane_at, 4), 4)
            piece = turned_gaps[shift, pl.ds(q % 2 * 4 + plane_at // 4, 1), :]
            line = jnp.where(quarter == q, piece, line)
        for w in range(NW):
            weights[w, pl.ds(b, 1), :] = (
                -4.0 * line / ((line * line + freqs[w] * freqs[w]) * math.sqrt(pairs))
            )

    bufs = (lent, own)

    def begin(buf, parts, start):
        width = buf.shape[-1]
        for h in range(2):
            part = parts[h * ncol:(h + 1) * ncol, :, start:start + width]
            buf[0, h] = part.reshape(2 * ncol, width)

    def place(way, s):
        return 0 if s == 0 else nz - 1 if s == half else 2 * s - 1 + way

    def push(first, count):
        late = int(first > EARLY)
        for n in range(2):
            remote(
                lent.at[pl.ds(first, count)], got.at[hi, pl.ds(first, count)],
                xsend.at[n], xrecv.at[hi, late], side[n],
            ).start()

    def arrived(n, h, way, s):
        wait(bufs[n].at[place(way, s), h], zrecv.at[way, n, h, s - 1])

    def tick(n, s):
        for h in range(2):
            for way, device in ((0, up), (1, down)):
                if s > 0:
                    arrived(n, h, way, s)
                if s == half - 1 and way != h:
                    continue
                remote(
                    bufs[n].at[place(way, s), h], bufs[n].at[place(way, s + 1), h],
                    zsend.at[way, n, h], zrecv.at[way, n, h, s], device,
                ).start()

    def last(n):
        for h in range(2):
            arrived(n, h, h, half)

    def window_arrived(way, s):
        slab = win.at[place(way, s)]
        wait(slab.at[way] if s == half else slab, nrecv.at[way, s - 1])

    def window_tick(s):
        for way, device in ((0, up), (1, down)):
            if s > 0:
                window_arrived(way, s)
            src, dst = win.at[place(way, s)], win.at[place(way, s + 1)]
            if s == half - 1:
                src, dst = src.at[way], dst.at[way]
            remote(src, dst, nsend.at[way], nrecv.at[way, s], device).start()

    window_col = row // 2
    in_w = lax.rem(window_col, 4)
    same_core = core == lax.rem(in_w, 2)
    same_line = jnp.logical_and(same_core, lo == in_w // 2)
    is_source = jnp.logical_and(same_line, y == window_col // 4)

    def window_y():
        @pl.when(is_source)
        def _():
            for b in range(2):
                @pl.when(lax.rem(row, 2) == b)
                def _():
                    wbuf[...] = win[:, :, :, b * GSR:(b + 1) * GSR]
            for k, device in enumerate(in_column):
                remote(wbuf, wbuf, wsend.at[k], wrecv.at[0], device).start()

    def window_x():
        @pl.when(same_line)
        def _():
            @pl.when(jnp.logical_not(is_source))
            def _():
                wait(wbuf, wrecv.at[0])
            remote(wbuf, wbuf, wsend.at[ny - 1], wrecv.at[1], twin_lo).start()

    def window_core():
        @pl.when(same_core)
        def _():
            @pl.when(jnp.logical_not(same_line))
            def _():
                wait(wbuf, wrecv.at[1])
            remote(wbuf, wbuf, wsend.at[ny], wrecv.at[2], twin_core).start()

    def window_done():
        @pl.when(jnp.logical_not(same_core))
        def _():
            wait(wbuf, wrecv.at[2])

        @pl.loop(0, pairs // GSR)
        def _(b):
            at = pl.multiple_of(b * GSR, GSR)
            block = wbuf[pl.ds(b * 2, 2)].reshape(GSR, GSR)
            turned = block.astype(jnp.float32).T
            for w in range(NW):
                lhs[w * GSR:(w + 1) * GSR, pl.ds(at, GSR)] = (
                    turned * weights[w, pl.ds(b, 1), :]
                ).astype(jnp.bfloat16)

    early = EARLY * 4 * ncol

    def product(panel, low, high):
        return jnp.dot(
            lhs[:, low:high], panel.reshape(high - low, panel.shape[-1]), preferred_element_type=jnp.float32
        )

    def finish(chi, to, at, sem):
        to[...] = chi.astype(jnp.bfloat16).reshape(to.shape)
        write(to, at, sem).start()

    def write(to, at, sem):
        return pltpu.make_async_copy(to, out.at[:, :, pl.ds(at, to.shape[-1])], osem.at[sem])

    def lent_at(h):
        return pl.multiple_of(WINDOW + OWN + h * LENT, 128)

    wait(parts_a.at[pl.ds(0, plane - 1)], part_recv.at[0])
    begin(win, parts_a, 0)
    window_tick(0)
    begin(lent, parts_a, WINDOW)
    for t in range(half + 1):
        if 0 < t < half // 2:
            window_tick(2 * t)
        if t == half // 2:
            for way in range(2):
                window_arrived(way, half)
            window_y()
        if t < half:
            tick(0, t)
        else:
            last(0)
        push(*((0, 1) if t == 0 else (nz - 1, 1) if t == half else (place(0, t), 2)))
        if t == 0:
            for copy in packing[6:]:
                copy.wait()
            exchange(1)
        if t < half // 2:
            window_tick(2 * t + 1)
        if t == 1:
            wait(parts_b.at[pl.ds(0, plane - 1)], part_recv.at[1])
            begin(own, parts_b, 0)
        if t > 0:
            tick(1, t - 1)
        if t == half // 2 + 1:
            window_x()
        if t == half // 2 + 2:
            window_core()
        if t == half // 2 + 3:
            window_done()

    finish(product(win[...], 0, pairs), out_win, 0, 0)
    sum_own[...] = product(own[:EARLY], 0, early)

    @pl.loop(0, 2)
    def _(h):
        wait(got.at[h, pl.ds(0, EARLY + 1)], xrecv.at[h, 0])
        sum_got[h] = product(got[h, :EARLY], 0, early)

    last(1)
    finish(sum_own[...] + product(own[EARLY:], early, pairs), out_own, WINDOW, 1)

    @pl.loop(0, 2)
    def _(h):
        wait(got.at[h, pl.ds(EARLY + 1, nz - EARLY - 1)], xrecv.at[h, 1])
        finish(sum_got[h] + product(got[h, EARLY:], early, pairs), out_got.at[h], lent_at(h), 2 + h)

    for way in range(2):
        wait(win.at[pl.ds(0, nz - 1), 0], nsend.at[way])
        for n in range(2):
            for h in range(2):
                wait(bufs[n].at[pl.ds(0, half if way == h else half - 1), h], zsend.at[way, n, h])
    for n in range(2):
        wait(lent, xsend.at[n])
    for n, parts in enumerate((parts_a, parts_b)):
        wait(parts.at[pl.ds(0, plane - 1)], part_send.at[n])

    @pl.when(is_source)
    def _():
        for k in range(ny - 1):
            wait(wbuf, wsend.at[k])

    @pl.when(same_line)
    def _():
        wait(wbuf, wsend.at[ny - 1])

    @pl.when(same_core)
    def _():
        wait(wbuf, wsend.at[ny])

    write(out_win, 0, 0).wait()
    write(out_own, WINDOW, 1).wait()
    for h in range(2):
        write(out_got.at[h], lent_at(h), 2 + h).wait()


def on_device(pair_elements, energy_gaps, frequencies):
    rows, cols = lax.axis_size("row"), lax.axis_size("col")
    local, full = pair_elements.shape
    pairs = local * rows * cols
    block = full // cols
    nz, ny = rows // 2, cols // 4
    depth = local * cols
    plane = 2 * cols
    dma = pltpu.SemaphoreType.DMA

    def panels(width):
        return pltpu.VMEM((nz, 2, depth, width), jnp.bfloat16)

    def results(width):
        return pltpu.VMEM((NW, GSR, width), jnp.bfloat16)

    operands = [
        pltpu.with_memory_space_constraint(operand, pltpu.HBM)
        for operand in (
            pair_elements.reshape(local, ny, 2, 2, block).transpose(1, 2, 3, 0, 4),
            energy_gaps.reshape(pairs // GSR, GSR),
            frequencies,
        )
    ]
    return pl.pallas_call(
        functools.partial(kernel, nz, ny, pairs),
        out_shape=jax.ShapeDtypeStruct((NW, GSR, block), jnp.bfloat16),
        in_specs=[pl.BlockSpec(memory_space=pl.ANY)] * 3,
        out_specs=pl.BlockSpec(memory_space=pl.ANY),
        scratch_shapes=[
            pltpu.VMEM((pairs // GSR, GSR), jnp.float32),
            pltpu.VMEM((4, pairs // GSR, GSR), jnp.float32),
            pltpu.VMEM((NW, pairs // GSR, GSR), jnp.float32),
            pltpu.SMEM((NW,), jnp.float32),
            pltpu.VMEM((2, ny, 2, 2, local, WINDOW + LENT), jnp.bfloat16),
            pltpu.VMEM((2, ny, 2, 2, local, OWN), jnp.bfloat16),
            pltpu.VMEM((plane, local, WINDOW + LENT), jnp.bfloat16),
            pltpu.VMEM((plane, local, OWN), jnp.bfloat16),
            panels(WINDOW),
            panels(OWN),
            panels(LENT),
            pltpu.VMEM((2, nz, 2, depth, LENT), jnp.bfloat16),
            panels(GSR),
            pltpu.VMEM((NW * GSR, pairs), jnp.bfloat16),
            pltpu.VMEM((NW * GSR, OWN), jnp.float32),
            pltpu.VMEM((2, NW * GSR, LENT), jnp.float32),
            results(WINDOW),
            results(OWN),
            pltpu.VMEM((2, NW, GSR, LENT), jnp.bfloat16),
            dma((2,)),
            dma((8,)),
            dma((2,)),
            dma((2,)),
            dma((2, nz // 2)),
            dma((2,)),
            dma((2, 2, 2, nz // 2)),
            dma((2, 2, 2)),
            dma((2, 2)),
            dma((2,)),
            dma((3,)),
            dma((ny + 1,)),
            dma((4,)),
        ],
        compiler_params=pltpu.CompilerParams(
            collective_id=0, has_side_effects=True, vmem_limit_bytes=36 * 1024 * 1024
        ),
        cost_estimate=pl.CostEstimate(
            flops=2 * NW * GSR * pairs * block, bytes_accessed=2 * NW * GSR * block, transcendentals=0
        ),
    )(*operands)


def solution(mesh):
    in_specs = (P(("row", "col"), None), P(), P())
    out_specs = P(None, "row", "col")
    return jax.shard_map(
        on_device, mesh=mesh, in_specs=in_specs, out_specs=out_specs, check_vma=False
    )
```

time: 86.4 us -> 85.1 us (0.985)
  the two profiles are of different devices: /device:TPU:32 before, /device:TPU:1 now
where the time goes in v1:
time: 85.1 us; the launch traced here: 84.1 us
  Pallas kernels  82.5 us (97%)
  local copies, waits for them, and re-layouts  1.6 us (2%)
    pallas_call x1, Pallas kernels, on_device(): pl.pallas_call(functools.partial(kernel, nz, ny, pairs), out_shape=jax.Sh...  82.5 us

profile of v1, /device:TPU:1, one launch (start us, length us, event | category | flops | bytes accessed | tf_op | source)
XLA Modules:
  0.0 84.1 jit_solution(4141370867956306673)
XLA Ops:
  0.0 82.5 %shard_map.37 = bf16[3,128,3840]{2,1,0:T(8,128)(2,1)S(1)} custom-call(bf16[4,2,2,2,3840]{4,3,2,1,0:T(2,128)(2,1)} %bitcast.4, f32[8,128]{1,0:T(8,128)} %bitcast.5, f32[3]{0:T(128)} %freqs_in.1), custom_call_target="tpu_custom_call" | custom-call | flops 3019898880 | bytes 2949120 | tf_op jit(solution)/shard_map/pallas_call | solution.py:341
  82.5 1.6 %copy.5 = bf16[3,128,3840]{2,1,0:T(8,128)(2,1)} copy(bf16[3,128,3840]{2,1,0:T(8,128)(2,1)S(1)} %shard_map.37) | data formatting | bytes 5898240

commit v2 on v1

--- a/solution.py
+++ b/solution.py
@@ -38,9 +38,9 @@
     twin_core = (row, y * 4 + lo * 2 + (1 - core))
     half = nz // 2
 
-    def seated(k):
-        to = lax.rem(seat + k, plane)
-        return to // ncol, lax.rem(to, ncol) // 4, lax.rem(to, 4) // 2, lax.rem(to, 2)
+    def seated(h, k):
+        c = lax.rem(col + k, ncol)
+        return h, c // 4, lax.rem(c, 4) // 2, lax.rem(c, 2)
 
     def device_at(h, y, lo, core):
         return h * nz + z, y * 4 + lo * 2 + core
@@ -49,9 +49,11 @@
     for device in (up, down):
         pl.semaphore_signal(barrier, inc=1, device_id=device, device_id_type=MESH)
 
-    @pl.loop(1, plane)
-    def _(k):
-        pl.semaphore_signal(barrier, inc=1, device_id=device_at(*seated(k)), device_id_type=MESH)
+    def for_others(do):
+        pl.loop(1, ncol)(lambda k: do(seated(hi, k)))
+        pl.loop(0, ncol)(lambda k: do(seated(1 - hi, k)))
+
+    for_others(lambda to: pl.semaphore_signal(barrier, inc=1, device_id=device_at(*to), device_id_type=MESH))
 
     packing = []
     for h in range(2):
@@ -92,12 +94,14 @@
     def exchange(n):
         packed, parts = ((packed_a, parts_a), (packed_b, parts_b))[n]
 
-        @pl.loop(1, plane)
-        def _(k):
-            to = seated(k)
-            remote(packed.at[to], parts.at[seat], part_send.at[n], part_recv.at[n], device_at(*to)).start()
-
+        for_others(lambda to: remote(
+            packed.at[to], parts.at[seat], part_send.at[n], part_recv.at[n, hi], device_at(*to)
+        ).start())
         parts[seat] = packed[hi, y, lo, core]
+
+    def exchanged(n, same):
+        parts = (parts_a, parts_b)[n]
+        wait(parts.at[pl.ds(0, ncol - 1 if same else ncol)], part_recv.at[n, hi if same else 1 - hi])
 
     exchange(0)
 
@@ -122,11 +126,10 @@
 
     bufs = (lent, own)
 
-    def begin(buf, parts, start):
+    def begin(buf, h, parts, start):
         width = buf.shape[-1]
-        for h in range(2):
-            part = parts[h * ncol:(h + 1) * ncol, :, start:start + width]
-            buf[0, h] = part.reshape(2 * ncol, width)
+        part = parts[pl.ds(pl.multiple_of(h * ncol, ncol), ncol), :, start:start + width]
+        buf[0, h] = part.reshape(2 * ncol, width)
 
     def place(way, s):
         return 0 if s == 0 else nz - 1 if s == half else 2 * s - 1 + way
@@ -142,8 +145,8 @@
     def arrived(n, h, way, s):
         wait(bufs[n].at[place(way, s), h], zrecv.at[way, n, h, s - 1])
 
-    def tick(n, s):
-        for h in range(2):
+    def tick(n, s, lanes=(0, 1)):
+        for h in lanes:
             for way, device in ((0, up), (1, down)):
                 if s > 0:
                     arrived(n, h, way, s)
@@ -235,12 +238,20 @@
     def lent_at(h):
         return pl.multiple_of(WINDOW + OWN + h * LENT, 128)
 
-    wait(parts_a.at[pl.ds(0, plane - 1)], part_recv.at[0])
-    begin(win, parts_a, 0)
+    for same, h in ((True, hi), (False, 1 - hi)):
+        exchanged(0, same)
+        begin(lent, h, parts_a, WINDOW)
+        tick(0, 0, (h,))
+    for h in range(2):
+        begin(win, h, parts_a, 0)
     window_tick(0)
-    begin(lent, parts_a, WINDOW)
-    for t in range(half + 1):
-        if 0 < t < half // 2:
+    push(0, 1)
+    for copy in packing[6:]:
+        copy.wait()
+    exchange(1)
+    window_tick(1)
+    for t in range(1, half + 1):
+        if t < half // 2:
             window_tick(2 * t)
         if t == half // 2:
             for way in range(2):
@@ -248,29 +259,28 @@
             window_y()
         if t < half:
             tick(0, t)
+            push(place(0, t), 2)
         else:
             last(0)
-        push(*((0, 1) if t == 0 else (nz - 1, 1) if t == half else (place(0, t), 2)))
-        if t == 0:
-            for copy in packing[6:]:
-                copy.wait()
-            exchange(1)
+            push(nz - 1, 1)
         if t < half // 2:
             window_tick(2 * t + 1)
-        if t == 1:
-            wait(parts_b.at[pl.ds(0, plane - 1)], part_recv.at[1])
-            begin(own, parts_b, 0)
-        if t > 0:
-            tick(1, t - 1)
         if t == half // 2 + 1:
             window_x()
+        if t == half // 2 + 3:
+            window_done()
+        if t == 1:
+            for same, h in ((True, hi), (False, 1 - hi)):
+                exchanged(1, same)
+                begin(own, h, parts_b, 0)
+                tick(1, 0, (h,))
+        else:
+            tick(1, t - 1)
         if t == half // 2 + 2:
             window_core()
         if t == half // 2 + 3:
-            window_done()
-
-    finish(product(win[...], 0, pairs), out_win, 0, 0)
-    sum_own[...] = product(own[:EARLY], 0, early)
+            finish(product(win[...], 0, pairs), out_win, 0, 0)
+            sum_own[...] = product(own[:EARLY], 0, early)
 
     @pl.loop(0, 2)
     def _(h):
@@ -365,7 +375,7 @@
             pltpu.VMEM((2, NW, GSR, LENT), jnp.bfloat16),
             dma((2,)),
             dma((8,)),
-            dma((2,)),
+            dma((2, 2)),
             dma((2,)),
             dma((2, nz // 2)),
             dma((2,)),

time: 85.1 us -> 86.9 us (1.021)
  the two profiles are of different devices: /device:TPU:1 before, /device:TPU:2 now
where the time goes in v2:
time: 86.9 us; the launch traced here: 86.7 us
  Pallas kernels  85.1 us (98%)
  local copies, waits for them, and re-layouts  1.6 us (2%)
    pallas_call x1, Pallas kernels, on_device(): pl.pallas_call(functools.partial(kernel, nz, ny, pairs), out_shape=jax.Sh...  85.1 us

profile of v2, /device:TPU:2, one launch (start us, length us, event | category | flops | bytes accessed | tf_op | source)
XLA Modules:
  0.0 86.7 jit_solution(3050645153561925786)
XLA Ops:
  0.0 85.1 %shard_map.37 = bf16[3,128,3840]{2,1,0:T(8,128)(2,1)S(1)} custom-call(bf16[4,2,2,2,3840]{4,3,2,1,0:T(2,128)(2,1)} %bitcast.4, f32[8,128]{1,0:T(8,128)} %bitcast.5, f32[3]{0:T(128)} %freqs_in.1), custom_call_target="tpu_custom_call" | custom-call | flops 3019898880 | bytes 2949120 | tf_op jit(solution)/shard_map/pallas_call | solution.py:351
  85.1 1.6 %copy.5 = bf16[3,128,3840]{2,1,0:T(8,128)(2,1)} copy(bf16[3,128,3840]{2,1,0:T(8,128)(2,1)S(1)} %shard_map.37) | data formatting | bytes 5898240
